TPU v7x, 32 devices: a whole 2x2x4 slice. The times are simulated.
32 devices in a mesh: ctx: 4 (over y, core), head: 8 (over z, x).
Axes of the slice: x: 2, y: 2, z: 4, core: 2. Of those that a mesh axis runs over, the one named last changes fastest.
Arguments:
- tokens: bfloat16 [4096, 2048], P('ctx', 'head'), may hold values from -6 to 6
- beta: float32 [4096, 8], P('ctx', 'head'), may hold values from 0 to 2
- w_query: bfloat16 [2048, 1024], P(None, 'head'), may hold values from -0.125 to 0.125
- w_key: bfloat16 [2048, 1024], P(None, 'head'), may hold values from -0.125 to 0.125
- w_value: bfloat16 [2048, 1024], P(None, 'head'), may hold values from -0.125 to 0.125
- gain: float32 [128], replicated, may hold values from 0.25 to 1.75
- w_out: bfloat16 [1024, 2048], P('head'), may hold values from -0.1875 to 0.1875
Outputs:
- mixed: bfloat16 [4096, 2048], P(('ctx', 'head'))
All inputs are finite; a program needn't handle non-finite values.
Results may differ from a plain program's by a relative error of at most 0.023.
Values may be sent and summed in bfloat16 or wider, within the bound.
A program may use at most 64 MiB of HBM per device.

v0:
```python
import jax
import jax.numpy as jnp
from jax import lax
from jax.sharding import PartitionSpec as P

DK = 128
BLOCK = 64


def passed_along(value, axis, steps):
    count = lax.axis_size(axis)
    first, last = (max(0, -steps), min(count, count - steps))
    return lax.ppermute(value, axis, [(source, source + steps) for source in range(first, last)])


def matmul(left, right):
    return jnp.dot(left, right, precision=lax.Precision.HIGHEST, preferred_element_type=jnp.float32)


def unit_rows(matrix):
    return matrix * lax.rsqrt(jnp.sum(matrix * matrix, axis=-1, keepdims=True) + 1e-06)


def block_factors(block_key, block_value, block_rate):
    lower_tri = jnp.tril(block_rate[:, None] * matmul(block_key, block_key.T), -1) + jnp.eye(
        BLOCK, dtype=jnp.float32
    )
    key_factor = jax.scipy.linalg.solve_triangular(
        lower_tri, block_rate[:, None] * block_key, lower=True, unit_diagonal=True
    )
    value_factor = jax.scipy.linalg.solve_triangular(
        lower_tri, block_rate[:, None] * block_value, lower=True, unit_diagonal=True
    )
    return (key_factor, value_factor)


def shard_transition(keys, value_rows, rates):
    count = keys.shape[0] // BLOCK
    block_keys = keys.reshape(count, BLOCK, DK)
    key_factor, value_factor = jax.vmap(block_factors)(
        block_keys, value_rows.reshape(count, BLOCK, DK), rates.reshape(count, BLOCK)
    )
    identity_mat = jnp.eye(DK, dtype=jnp.float32)
    block_mult = identity_mat - jnp.einsum(
        "nck,ncj->nkj", key_factor, block_keys, precision=lax.Precision.HIGHEST
    )
    block_add = jnp.einsum(
        "ncv,nck->nvk", value_factor, block_keys, precision=lax.Precision.HIGHEST
    )

    def compose(carried, block_map):
        multiplier, addend = carried
        next_mult, next_add = block_map
        return ((matmul(multiplier, next_mult), matmul(addend, next_mult) + next_add), None)

    start_pair = (identity_mat, jnp.zeros((DK, DK), jnp.float32))
    (multiplier, addend), _ = lax.scan(compose, start_pair, (block_mult, block_add))
    return (key_factor, value_factor, multiplier, addend)


def shard_outputs(queries, keys, key_factor, value_factor, memory_state):
    count = keys.shape[0] // BLOCK

    def advance(current, block_data):
        block_query, block_key, block_kf, block_vf = block_data
        written = block_vf - matmul(block_kf, current.T)
        output_rows = matmul(block_query, current.T) + matmul(
            jnp.tril(matmul(block_query, block_key.T)), written
        )
        return (current + matmul(written.T, block_key), output_rows)

    blocked = (
        queries.reshape(count, BLOCK, DK),
        keys.reshape(count, BLOCK, DK),
        key_factor,
        value_factor,
    )
    _, outputs = lax.scan(advance, memory_state, blocked)
    return outputs.reshape(count * BLOCK, DK)


def local(tokens, beta, w_query, w_key, w_value, gain, w_out):
    tok_rows = tokens.shape[0]
    head_width = w_query.shape[1]
    heads_here = beta.shape[1]
    portion = lax.all_gather(tokens, "head", axis=1, tiled=True)
    raw_query, raw_key, raw_value = tuple(
        (
            jnp.dot(portion, weight, preferred_element_type=jnp.float32)
            for index, weight in enumerate((w_query, w_key, w_value))
        )
    )

    def split_heads(matrix):
        return matrix.reshape(tok_rows, heads_here, DK).transpose(1, 0, 2)

    queries = unit_rows(jax.nn.silu(split_heads(raw_query)))
    keys = unit_rows(jax.nn.silu(split_heads(raw_key)))
    value_rows = split_heads(raw_value)
    key_factor, value_factor, multiplier, addend = jax.vmap(shard_transition)(
        keys, value_rows, beta.T
    )

    def relay_turn(counter, carried):
        incoming, outgoing = carried
        incoming = passed_along(outgoing.astype(jnp.bfloat16), "ctx", 1).astype(outgoing.dtype)
        outgoing = (
            jnp.einsum("hij,hjk->hik", incoming, multiplier, precision=lax.Precision.HIGHEST)
            + addend
        )
        return (incoming, outgoing)

    state_in, _ = lax.fori_loop(
        0, lax.axis_size("ctx") - 1, relay_turn, (jnp.zeros_like(addend), addend)
    )
    recurrent = jax.vmap(shard_outputs)(queries, keys, key_factor, value_factor, state_in)
    scale_inv = lax.rsqrt(jnp.mean(recurrent * recurrent, axis=-1, keepdims=True) + 1e-05)
    normed = (recurrent * scale_inv * gain).astype(jnp.bfloat16)
    normed = normed.transpose(1, 0, 2).reshape(tok_rows, head_width)
    portion = normed
    return lax.psum_scatter(
        jnp.dot(portion, w_out, preferred_element_type=jnp.float32).astype(jnp.bfloat16),
        "head",
        scatter_dimension=0,
        tiled=True,
    )


def solution(mesh):
    placed = (
        P("ctx", "head"),
        P("ctx", "head"),
        P(None, "head"),
        P(None, "head"),
        P(None, "head"),
        P(),
        P("head", None),
    )
    return jax.shard_map(
        local, mesh=mesh, in_specs=placed, out_specs=P(("ctx", "head"), None), check_vma=False
    )
```

profile of v0, /device:TPU:0, one launch (start us, length us, event | category | flops | bytes accessed | tf_op | source)
XLA Modules:
  0.0 406.5 jit_solution(1149261543981123071)
XLA Ops:
  7.8 1.3 reduce.9
  9.3 77.9 %all-gather.2.cloned.1.call-done = bf16[1024,2048]{1,0:T(8,128)(2,1)} async-done(((bf16[1024,256]{1,0:T(8,128)(2,1)}), bf16[1024,2048]{1,0:T(8,128)(2,1)}) %all-gather.2.cloned.1.call-update) | async-done | bytes 4194320 | tf_op jit(solution)/shard_map/all_gather | solution.py:86
  87.2 3.8 multiply_reduce_fusion.2
  91.0 2.1 multiply_reduce_fusion.1
  94.2 78.8 %custom-call.4 = f32[1,16,1,64,64]{3,4,2,1,0:T(8,128)S(1)} custom-call(f32[1,16,1,64,64]{4,3,2,1,0:T(8,128)S(1)} %fusion.39), custom_call_target="InvertDiagBlocksLowerTriangular" | custom-call | tf_op jit(solution)/shard_map/vmap(vmap(jit(_solve_triangular)))/triangular_solve | solution.py:28
  173.1 3.4 fusion.56
  176.5 1.1 fusion.42
  177.6 1.1 fusion.44
  178.8 2.8 convolution_bitcast_fusion.3
  181.6 1.8 fusion.33
  183.4 25.5 %while.36 = (s32[]{:T(128)}, f32[1,128,128]{1,2,0:T(8,128)S(1)}, f32[1,128,128]{1,2,0:T(8,128)S(1)}, f32[16,1,128,128]{3,2,1,0:T(8,128)S(1)}, f32[16,1,128,128]{3,2,0,1:T(8,128)}, /*index=5*/s32[]{:T(128)}) while((s32[]{:T(128)}, f32[1,128,128]{1,2,0:T(8,128)S(1)}, f32[1,128,128]{1,2,0:T(8,128)S(1)}, f32[16,1,128,128]{3,2,1,0:T(8,128)S(1)}, ...), condition=%wide.region_2.4_spmd, body=%wide.region_1.0_spmd.sunk | while | flops 50348032 | bytes 983129 | solution.py:57
  209.1 1.2 broadcast_multiply_fusion
  210.4 15.0 %while.37 = (s32[]{:T(128)}, f32[1,128,128]{2,1,0:T(8,128)}, bf16[1,128,128]{2,1,0:T(8,128)(2,1)S(1)}, f32[1,128,128]{2,1,0:T(8,128)S(1)}, f32[1,128,128]{2,1,0:T(8,128)S(1)}, /*index=5*/s32[]{:T(128)}) while((s32[]{:T(128)}, f32[1,128,128]{2,1,0:T(8,128)}, bf16[1,128,128]{2,1,0:T(8,128)(2,1)S(1)}, f32[1,128,128]{2,1,0:T(8,128)S(1)}, ...), condition=%wide.region_4.6_spmd, body=%wide.region_3.5_spmd.sunk | while | flops 25214976 | bytes 426093 | solution.py:113
  210.4 1.3 collective-permute-start
  213.4 4.3 %collective-permute-start = (bf16[1,128,128]{2,1,0:T(8,128)(2,1)S(1)}, bf16[1,128,128]{2,1,0:T(8,128)(2,1)S(1)}, u32[]{:S(2)}, u32[]{:S(2)}) collective-permute-start(bf16[1,128,128]{2,1,0:T(8,128)(2,1)S(1)} %get-tuple-element.287), channel_id=1, source_target_pairs={{0,8},{8,16},{16,24},{1,9},{9,17},{17,25},{2,10},{10,18},{18,26},{... | collective-permute-start | bytes 98312 | tf_op jit(solution)/shard_map/while/body/eval_jaxpr/ppermute | solution.py:13
  219.3 4.4 %collective-permute-start = (bf16[1,128,128]{2,1,0:T(8,128)(2,1)S(1)}, bf16[1,128,128]{2,1,0:T(8,128)(2,1)S(1)}, u32[]{:S(2)}, u32[]{:S(2)}) collective-permute-start(bf16[1,128,128]{2,1,0:T(8,128)(2,1)S(1)} %get-tuple-element.287), channel_id=1, source_target_pairs={{0,8},{8,16},{16,24},{1,9},{9,17},{17,25},{2,10},{10,18},{18,26},{... | collective-permute-start | bytes 98312 | tf_op jit(solution)/shard_map/while/body/eval_jaxpr/ppermute | solution.py:13
  225.4 78.5 %while.38 = (s32[]{:T(128)}, f32[1,128,128]{2,1,0:T(8,128)}, f32[16,1,64,128]{3,2,1,0:T(8,128)}, f32[16,1,64,128]{3,2,1,0:T(8,128)S(1)}, f32[16,1,64,128]{3,2,1,...) while((s32[]{:T(128)}, f32[1,128,128]{2,1,0:T(8,128)}, ...), condition=%wide.region_7.9_spmd, body=%wide.region_6.8_spmd.sunk | while | flops 50372608 | bytes 690281 | solution.py:78
  225.4 1.1 convolution_subtract_fusion.3
  226.5 1.1 fusion.114
  227.8 1.8 fusion.113
  230.3 1.1 convolution_subtract_fusion.3
  231.4 1.1 fusion.114
  232.7 1.8 fusion.113
  235.2 1.1 convolution_subtract_fusion.3
  236.3 1.1 fusion.114
  237.6 1.8 fusion.113
  240.1 1.1 convolution_subtract_fusion.3
  241.2 1.1 fusion.114
  242.5 1.8 fusion.113
  245.0 1.1 convolution_subtract_fusion.3
  246.1 1.1 fusion.114
  247.4 1.8 fusion.113
  251.0 1.1 fusion.114
  252.3 1.8 fusion.113
  254.8 1.1 convolution_subtract_fusion.3
  255.9 1.1 fusion.114
  257.2 1.8 fusion.113
  260.8 1.1 fusion.114
  262.1 1.8 fusion.113
  264.6 1.1 convolution_subtract_fusion.3
  265.7 1.1 fusion.114
  267.0 1.8 fusion.113
  269.6 1.1 convolution_subtract_fusion.3
  270.6 1.1 fusion.114
  271.9 1.8 fusion.113
  275.5 1.1 fusion.114
  276.8 1.8 fusion.113
  279.4 1.1 convolution_subtract_fusion.3
  280.4 1.1 fusion.114
  281.7 1.8 fusion.113
  284.3 1.1 convolution_subtract_fusion.3
  285.3 1.1 fusion.114
  286.6 1.8 fusion.113
  289.2 1.1 convolution_subtract_fusion.3
  290.3 1.1 fusion.114
  291.5 1.8 fusion.113
  295.2 1.1 fusion.114
  296.4 1.8 fusion.113
  300.1 1.1 fusion.114
  301.3 1.8 fusion.113
  303.9 1.2 multiply_reduce_fusion
  305.2 1.2 fusion.41
  306.5 3.2 convolution_convert_fusion
  309.7 90.0 %reduce-scatter.2.cloned.1.call-done = bf16[128,2048]{1,0:T(8,128)(2,1)} async-done(((bf16[1024,2048]{1,0:T(8,128)(2,1)}), bf16[128,2048]{1,0:T(8,128)(2,1)}) %reduce-scatter.2.cloned.1.call-update) | async-done | bytes 524304 | tf_op jit(solution)/shard_map/reduce_scatter | solution.py:121
  (175 shorter events, 53.3 us)
Async XLA Ops:
  6.5 299.9 %copy-start = (bf16[128,2048]{1,0:T(8,128)(2,1)S(1)}, bf16[128,2048]{1,0:T(8,128)(2,1)}, u32[]{:S(2)}) copy-start(bf16[128,2048]{1,0:T(8,128)(2,1)} %param.21) | copy-start | bytes 1572868
  6.5 80.6 %all-gather.2.cloned.1.call-start = ((), (), s32[]{:S(2)}) async-start(), calls=%async_computation.1 | async-start | bytes 4718592 | tf_op jit(solution)/shard_map/all_gather | solution.py:86
  7.3 392.4 %reduce-scatter.2.cloned.1.call-start = ((), (), s32[]{:S(2)}) async-start(), calls=%async_computation.2 | async-start | bytes 4718592 | tf_op jit(solution)/shard_map/reduce_scatter | solution.py:121
  9.3 81.7 %copy-start.4 = (bf16[2048,128]{1,0:T(8,128)(2,1)S(1)}, bf16[2048,128]{1,0:T(8,128)(2,1)}, u32[]{:S(2)}) copy-start(bf16[2048,128]{1,0:T(8,128)(2,1)} %param.17) | copy-start | bytes 1572868
  87.2 3.8 copy-start.1
  91.0 82.1 %copy-start.2 = (bf16[2048,128]{1,0:T(8,128)(2,1)S(1)}, bf16[2048,128]{1,0:T(8,128)(2,1)}, u32[]{:S(2)}) copy-start(bf16[2048,128]{1,0:T(8,128)(2,1)} %param.19) | copy-start | bytes 1572868
  208.9 96.3 %copy-start.3 = (f32[128]{0:T(128)S(1)}, f32[128]{0:T(128)}, u32[]{:S(2)}) copy-start(f32[128]{0:T(128)} %param.20) | copy-start | bytes 1540
  210.4 2.2 collective-permute-start
  213.4 5.1 %collective-permute-start = (bf16[1,128,128]{2,1,0:T(8,128)(2,1)S(1)}, bf16[1,128,128]{2,1,0:T(8,128)(2,1)S(1)}, u32[]{:S(2)}, u32[]{:S(2)}) collective-permute-start(bf16[1,128,128]{2,1,0:T(8,128)(2,1)S(1)} %get-tuple-element.287), channel_id=1, source_target_pairs={{0,8},{8,16},{16,24},{1,9},{9,17},{17,25},{2,10},{10,18},{18,26},{... | collective-permute-start | bytes 98312 | tf_op jit(solution)/shard_map/while/body/eval_jaxpr/ppermute | solution.py:13
  219.3 5.2 %collective-permute-start = (bf16[1,128,128]{2,1,0:T(8,128)(2,1)S(1)}, bf16[1,128,128]{2,1,0:T(8,128)(2,1)S(1)}, u32[]{:S(2)}, u32[]{:S(2)}) collective-permute-start(bf16[1,128,128]{2,1,0:T(8,128)(2,1)S(1)} %get-tuple-element.287), channel_id=1, source_target_pairs={{0,8},{8,16},{16,24},{1,9},{9,17},{17,25},{2,10},{10,18},{18,26},{... | collective-permute-start | bytes 98312 | tf_op jit(solution)/shard_map/while/body/eval_jaxpr/ppermute | solution.py:13
Sparse Core Ops, SparseCore 0:
  9.4 77.7 all-gather.1
  309.8 89.8 reduce-scatter.1
where the time goes:
time: 410 us; the launch traced here: 407 us
  waiting for transfers between devices  171 us (42%)
  matrix products  108 us (26%)
  other arithmetic  86 us (21%)
  local copies, waits for them, and re-layouts  16.1 us (4%)
  between operations  13.6 us (3%)
  starting transfers between devices  10 us (2%)
    reduce_scatter x1, waiting for transfers between devices, local(): lax.psum_scatter(jnp.dot(portion, w_out, preferred_element_type=jnp.float...  90 us
    dot_general x113, matrix products, matmul(): jnp.dot(left, right, precision=lax.Precision.HIGHEST, preferred_element_t...  88.4 us
    another operation x4, other arithmetic, block_factors(): jax.scipy.linalg.solve_triangular(lower_tri, block_rate[:, None] * block_...  78.9 us
    all_gather x1, waiting for transfers between devices, local(): portion = lax.all_gather(tokens, 'head', axis=1, tiled=True)  77.9 us
    dynamic_slice x32, local copies, waits for them, and re-layouts, shard_transition(): lax.scan(compose, start_pair, (block_mult, block_add))  15 us
    ppermute x3, starting transfers between devices, passed_along(): lax.ppermute(value, axis, [(source, source + steps) for source in range(f...  9.96 us
    dot_general x3, matrix products, local(): jnp.dot(portion, weight, preferred_element_type=jnp.float32)  9.27 us
  transfers between devices with their start and end apart: 5, of which 5 were waited for; matrix products, arithmetic and copies ran while one was open for 0% of the time, Pallas kernels for 0%

commit v1 on v0

v1 whole, which is shorter than its diff:
```python
import functools

import jax
import jax.numpy as jnp
from jax import lax
from jax.experimental import pallas as pl
from jax.experimental.pallas import tpu as pltpu
from jax.sharding import PartitionSpec as P

DK = 128
CHUNK = 128
F32, BF16 = jnp.float32, jnp.bfloat16


def dot(left, right):
    return jnp.dot(left.astype(BF16), right.astype(BF16), preferred_element_type=F32)


def dot_nt(left, right):
    return lax.dot_general(
        left.astype(BF16), right.astype(BF16), (((1,), (1,)), ((), ())), preferred_element_type=F32
    )


def dot_tn(left, right):
    return lax.dot_general(
        left.astype(BF16), right.astype(BF16), (((0,), (0,)), ((), ())), preferred_element_type=F32
    )


def unit_silu(raw):
    act = raw / (1.0 + jnp.exp(-raw))
    return act * lax.rsqrt(jnp.sum(act * act, axis=-1, keepdims=True) + 1e-6)


def unit_lower_inverses(lowers):
    size = lowers[0].shape[0]
    row = lax.broadcasted_iota(jnp.int32, (size, size), 0)
    col = lax.broadcasted_iota(jnp.int32, (size, size), 1)
    inverses = None
    level = 0
    while (1 << level) < size:
        mask = (
            ((row >> (level + 1)) == (col >> (level + 1)))
            & (((row >> level) & 1) == 1)
            & (((col >> level) & 1) == 0)
        )
        parts = [jnp.where(mask, lower, 0.0) for lower in lowers]
        if inverses is None:
            eye = jnp.where(row == col, 1.0, 0.0)
            inverses = [eye - part for part in parts]
        else:
            halves = [dot(inverse, part) for inverse, part in zip(inverses, parts)]
            inverses = [
                inverse - dot(half, inverse) for inverse, half in zip(inverses, halves)
            ]
        level += 1
    return inverses


def shard_maps(raw, rates, emit):
    count = len(raw)
    row = lax.broadcasted_iota(jnp.int32, (CHUNK, CHUNK), 0)
    col = lax.broadcasted_iota(jnp.int32, (CHUNK, CHUNK), 1)
    queries = [unit_silu(raw[i][0]) for i in range(count)]
    keys = [unit_silu(raw[i][1]) for i in range(count)]
    lowers = [
        jnp.where(row > col, rates[i] * dot_nt(keys[i], keys[i]), 0.0) for i in range(count)
    ]
    inverses = unit_lower_inverses(lowers)
    factors = [
        dot(inverses[i], jnp.concatenate([rates[i] * keys[i], rates[i] * raw[i][2]], axis=1))
        for i in range(count)
    ]
    moves = [dot_tn(keys[i], factors[i]) for i in range(count)]
    reads = [
        dot(jnp.where(row >= col, dot_nt(queries[i], keys[i]), 0.0), factors[i])
        for i in range(count)
    ]
    zero = jnp.zeros((DK, DK), F32)
    state = jnp.concatenate([jnp.where(row == col, 1.0, 0.0), zero], axis=1)
    for i in range(count):
        from_state = dot(queries[i] - reads[i][:, :DK], state)
        emit(i, from_state[:, :DK], from_state[:, DK:] + reads[i][:, DK:])
        state = (
            state
            - dot(moves[i][:, :DK], state)
            + jnp.concatenate([zero, moves[i][:, DK:]], axis=1)
        )
    return state


def shard_kernel(x_ref, w_ref, beta_ref, state_ref, query_ref, own_ref, raw_ref):
    count = x_ref.shape[0] // CHUNK

    def project(i, carry):
        rows = pl.ds(pl.multiple_of(i * CHUNK, CHUNK), CHUNK)
        raw_ref[rows, :] = jnp.dot(x_ref[rows, :], w_ref[...], preferred_element_type=F32)
        return carry

    lax.fori_loop(0, count, project, 0)

    def emit(i, query, own):
        rows = pl.ds(i * CHUNK, CHUNK)
        query_ref[rows, :] = query.astype(BF16)
        own_ref[rows, :] = own

    raw = [
        [raw_ref[pl.ds(i * CHUNK, CHUNK), pl.ds(j * DK, DK)] for j in range(3)]
        for i in range(count)
    ]
    rates = [beta_ref[pl.ds(i * CHUNK, CHUNK), :] for i in range(count)]
    state_ref[...] = shard_maps(raw, rates, emit).astype(BF16)


def normed_kernel(shards, states_ref, query_ref, own_ref, gain_ref, out_ref):
    me = lax.axis_index("ctx")
    start = jnp.zeros((DK, DK), F32)
    for shard in range(shards - 1):
        state = states_ref[shard]
        after = dot(state[:, :DK], start) + state[:, DK:].astype(F32)
        start = jnp.where(shard < me, after, start)
    recurrent = own_ref[...] + dot(query_ref[...], start)
    scale = lax.rsqrt(jnp.mean(recurrent * recurrent, axis=-1, keepdims=True) + 1e-5)
    out_ref[...] = (recurrent * scale * gain_ref[...]).astype(BF16)


def local(tokens, beta, w_query, w_key, w_value, gain, w_out):
    rows = tokens.shape[0]
    shards, heads = lax.axis_size("ctx"), lax.axis_size("head")
    whole = pl.BlockSpec(memory_space=pltpu.VMEM)
    portion = lax.all_gather(tokens, "head", axis=1, tiled=True)
    weights = jnp.concatenate([w_query, w_key, w_value], axis=1)
    state, query, own = pl.pallas_call(
        shard_kernel,
        out_shape=(
            jax.ShapeDtypeStruct((DK, 2 * DK), BF16),
            jax.ShapeDtypeStruct((rows, DK), BF16),
            jax.ShapeDtypeStruct((rows, DK), F32),
        ),
        in_specs=[whole] * 3,
        out_specs=(whole,) * 3,
        scratch_shapes=[pltpu.VMEM((rows, 3 * DK), F32)],
        compiler_params=pltpu.CompilerParams(vmem_limit_bytes=40 * 2**20),
    )(portion, weights, beta)
    states = lax.all_gather(state, "ctx")
    normed = pl.pallas_call(
        functools.partial(normed_kernel, shards),
        out_shape=jax.ShapeDtypeStruct((rows, DK), BF16),
        in_specs=[whole] * 4,
        out_specs=whole,
        compiler_params=pltpu.CompilerParams(vmem_limit_bytes=20 * 2**20),
    )(states, query, own, gain.reshape(1, DK))
    parts = lax.all_to_all(normed.reshape(heads, rows // heads, DK), "head", 0, 0)
    w_all = lax.all_gather(w_out, "head", axis=0, tiled=True)
    mixed_rows = parts.transpose(1, 0, 2).reshape(rows // heads, heads * DK)
    return jnp.dot(mixed_rows, w_all, preferred_element_type=F32).astype(BF16)


def solution(mesh):
    placed = (
        P("ctx", "head"),
        P("ctx", "head"),
        P(None, "head"),
        P(None, "head"),
        P(None, "head"),
        P(),
        P("head", None),
    )
    return jax.shard_map(
        local, mesh=mesh, in_specs=placed, out_specs=P(("ctx", "head"), None), check_vma=False
    )
```

time: 410 us -> 177 us (0.43)
  matrix products: 108 us -> 3.73 us
  other arithmetic: 86 us -> 1.57 us
  waiting for transfers between devices: 171 us -> 137 us
  local copies, waits for them, and re-layouts: 16.1 us -> 3.94 us
  Pallas kernels: 0 us -> 8.03 us
  starting transfers between devices: 10 us -> 3.45 us
  blocking collectives: 0 us -> 5.79 us
    dot_general x122 -> x1, matrix products: 106 us -> 3.73 us  [local(): return jnp.dot(mixed_rows, w_all, preferred_element_type=F32).astype(BF16)]
    reduce_scatter x1 -> x0, waiting for transfers between devices: 90 us -> none  [local(): lax.psum_scatter(jnp.dot(portion, w_out, preferred_element_type=jnp.float...]
    another operation x5 -> x0, other arithmetic: 78.9 us -> none  [the longest x4 78.9 us: block_factors(): jax.scipy.linalg.solve_triangular(lower_tri, block_rate[:, None] * block_...]
    all_gather x0 -> x1, waiting for transfers between devices: none -> 58.9 us  [local(): w_all = lax.all_gather(w_out, 'head', axis=0, tiled=True)]
    dynamic_slice x32 -> x0, local copies, waits for them, and re-layouts: 15 us -> none  [shard_transition(): lax.scan(compose, start_pair, (block_mult, block_add))]
    ppermute x3 -> x0, starting transfers between devices: 9.96 us -> none  [passed_along(): lax.ppermute(value, axis, [(source, source + steps) for source in range(f...]
    pallas_call x0 -> x2, Pallas kernels: none -> 8.03 us  [the longest x1 7.28 us: local(): pl.pallas_call(shard_kernel, out_shape=(jax.ShapeDtypeStruct((DK, 2 * DK)...]
    all_gather x0 -> x1, blocking collectives: none -> 5.79 us  [local(): states = lax.all_gather(state, 'ctx')]
  transfers between devices with their start and end apart: 5 -> 3, of which waited for: 5 -> 2; matrix products, arithmetic and copies ran while one was open for 0% -> 2% of each run, Pallas kernels for 0% -> 5%
where the time goes in v1:
time: 177 us
  waiting for transfers between devices  137 us (77%)
  between operations  13.4 us (8%)
  Pallas kernels  8.03 us (5%)
  blocking collectives  5.79 us (3%)
  local copies, waits for them, and re-layouts  3.94 us (2%)
  matrix products  3.73 us (2%)
  starting transfers between devices  3.45 us (2%)
    all_gather x1, waiting for transfers between devices, local(): portion = lax.all_gather(tokens, 'head', axis=1, tiled=True)  76.7 us
    all_gather x1, waiting for transfers between devices, local(): w_all = lax.all_gather(w_out, 'head', axis=0, tiled=True)  58.9 us
    pallas_call x1, Pallas kernels, local(): pl.pallas_call(shard_kernel, out_shape=(jax.ShapeDtypeStruct((DK, 2 * DK)...  7.28 us
    all_gather x1, blocking collectives, local(): states = lax.all_gather(state, 'ctx')  5.79 us
    dot_general x1, matrix products, local(): return jnp.dot(mixed_rows, w_all, preferred_element_type=F32).astype(BF16)  3.73 us
  transfers between devices with their start and end apart: 3, of which 2 were waited for; matrix products, arithmetic and copies ran while one was open for 2% of the time, Pallas kernels for 5%

profile of v1, /device:TPU:0, one launch (start us, length us, event | category | flops | bytes accessed | tf_op | source)
XLA Modules:
  0.0 176.9 jit_solution(7594435466988425465)
XLA Ops:
  6.5 0.0 all-gather.4.cloned.1.call-start
  6.5 0.7 all-gather.4.cloned.1.call-update
  7.3 0.0 all-gather.6.cloned.1.call-start
  7.3 0.7 all-gather.6.cloned.1.call-update
  8.0 0.9 copy.9.beta_ref
  8.9 1.6 pad_maximum_fusion.w_ref
  10.5 76.7 %all-gather.4.cloned.1.call-done.x_ref = bf16[1024,2048]{1,0:T(8,128)(2,1)} async-done(((bf16[1024,256]{1,0:T(8,128)(2,1)}), bf16[1024,2048]{1,0:T(8,128)(2,1)}) %all-gather.4.cloned.1.call-update) | async-done | bytes 4194320 | tf_op jit(solution)/shard_map/all_gather | solution.py:132
  87.1 0.0 copy-start
  87.2 2.2 %copy-done = bf16[1024,2048]{1,0:T(8,128)(2,1)S(1)} copy-done((bf16[1024,2048]{1,0:T(8,128)(2,1)S(1)}, bf16[1024,2048]{1,0:T(8,128)(2,1)}, u32[]{:S(2)}) %copy-start) | copy-done | bytes 4194328
  89.3 0.0 copy-start.1
  89.3 7.3 %shard_map.73 = (bf16[128,256]{1,0:T(8,128)(2,1)S(1)}, bf16[1024,128]{1,0:T(8,128)(2,1)S(1)}, f32[1024,128]{1,0:T(8,128)S(1)}) custom-call(bf16[1024,2048]{1,0:T(8,128)(2,1)S(1)} %copy-done, bf16[2048,384]{1,0:T(8,128)(2,1)S(1)} %pad_maximum_fusion.w_ref, f32[1024,1]{1,0:T(8,128)S(1)} %copy.9.beta_ref), custom_call_target="tpu_custom_call" | custom-call | tf_op jit(solution)/shard_map/pallas_call | solution.py:134
  96.6 5.8 %all-gather = bf16[512,256]{1,0:T(8,128)(2,1)S(1)} all-gather(bf16[128,256]{1,0:T(8,128)(2,1)S(1)} %get-tuple-element.8), channel_id=2, replica_groups=mesh['ctx'=4,'head'=8] {'ctx'}, dimensions={0}, use_global_device_ids=true | all-gather | bytes 327680 | tf_op jit(solution)/shard_map/all_gather | solution.py:146
  102.4 0.0 copy-done.1
  102.4 0.8 shard_map.74
  103.2 0.9 copy.10
  104.0 3.4 %all-to-all-start = ((bf16[8,128,128]{1,2,0:T(8,128)(2,1)}), bf16[8,128,128]{1,2,0:T(8,128)(2,1)S(1)}, u32[]{:S(2)}, u32[]{:S(2)}) async-start(bf16[8,128,128]{1,2,0:T(8,128)(2,1)} %copy.10), calls=%async_computation | async-start | bytes 524288 | tf_op jit(solution)/shard_map/all_to_all | solution.py:154
  107.4 58.9 %all-gather.6.cloned.1.call-done = bf16[1024,2048]{1,0:T(8,128)(2,1)} async-done(((bf16[128,2048]{1,0:T(8,128)(2,1)}), bf16[1024,2048]{1,0:T(8,128)(2,1)}) %all-gather.6.cloned.1.call-update) | async-done | bytes 4194320 | tf_op jit(solution)/shard_map/all_gather | solution.py:155
  166.3 0.0 all-to-all-done
  166.3 3.7 %convolution_convert_fusion = bf16[128,2048]{1,0:T(8,128)(2,1)} fusion(bf16[128,1024]{0,1:T(8,128)(2,1)S(1)} %bitcast.11, bf16[1024,2048]{1,0:T(8,128)(2,1)} %all-gather.6.cloned.1.call-done), kind=kOutput, calls=%fused_computation | convolution fusion | flops 537133056 | bytes 4980736 | tf_op jit(solution)/shard_map/dot_general | solution.py:157
Async XLA Ops:
  6.5 80.6 %all-gather.4.cloned.1.call-start = ((), (), s32[]{:S(2)}) async-start(), calls=%async_computation.1 | async-start | bytes 4718592 | tf_op jit(solution)/shard_map/all_gather | solution.py:132
  7.3 159.1 %all-gather.6.cloned.1.call-start = ((), (), s32[]{:S(2)}) async-start(), calls=%async_computation.2 | async-start | bytes 4718592 | tf_op jit(solution)/shard_map/all_gather | solution.py:155
  87.1 2.2 %copy-start = (bf16[1024,2048]{1,0:T(8,128)(2,1)S(1)}, bf16[1024,2048]{1,0:T(8,128)(2,1)}, u32[]{:S(2)}) copy-start(bf16[1024,2048]{1,0:T(8,128)(2,1)} %all-gather.4.cloned.1.call-done.x_ref) | copy-start | bytes 12582916
  89.3 13.1 %copy-start.1 = (f32[128]{0:T(128)S(1)}, f32[128]{0:T(128)}, u32[]{:S(2)}) copy-start(f32[128]{0:T(128)} %param.12) | copy-start | bytes 1540
  104.0 62.3 %all-to-all-start = ((bf16[8,128,128]{1,2,0:T(8,128)(2,1)}), bf16[8,128,128]{1,2,0:T(8,128)(2,1)S(1)}, u32[]{:S(2)}, u32[]{:S(2)}) async-start(bf16[8,128,128]{1,2,0:T(8,128)(2,1)} %copy.10), calls=%async_computation | async-start | bytes 524288 | tf_op jit(solution)/shard_map/all_to_all | solution.py:154
Sparse Core Ops, SparseCore 0:
  9.4 77.7 all-gather.3
  89.3 77.0 all-gather.5

commit v2 on v1

--- a/solution.py
+++ b/solution.py
@@ -90,71 +90,373 @@
     return state
 
 
-def shard_kernel(x_ref, w_ref, beta_ref, state_ref, query_ref, own_ref, raw_ref):
-    count = x_ref.shape[0] // CHUNK
-
-    def project(i, carry):
-        rows = pl.ds(pl.multiple_of(i * CHUNK, CHUNK), CHUNK)
-        raw_ref[rows, :] = jnp.dot(x_ref[rows, :], w_ref[...], preferred_element_type=F32)
-        return carry
-
-    lax.fori_loop(0, count, project, 0)
+class LineGather:
+    def __init__(self, own, slot, pieces, early, depth, width, sems, pending):
+        self.own, self.slot, self.pieces, self.early = own, slot, pieces, early
+        self.depth, self.width = depth, width
+        self.recv, self.up, self.down, self.cross = sems
+        self.pending = pending
+        me = lax.axis_index("head")
+        self.z, self.x = me // width, lax.rem(me, width)
+
+    def head(self, z, j=0):
+        return z * self.width + lax.rem(self.x + j, self.width)
+
+    def send(self, cond, source, shard, piece, sem, target):
+        def make():
+            return pltpu.make_async_remote_copy(
+                src_ref=source,
+                dst_ref=self.slot(shard, piece),
+                send_sem=sem,
+                recv_sem=self.recv.at[shard, piece],
+                device_id={"head": target},
+                device_id_type=pl.DeviceIdType.MESH,
+            )
+
+        guarded(cond, lambda: make().start())
+        self.pending.append((cond, make))
+
+    def arrive(self, shard, piece):
+        view = self.slot(shard, piece)
+        pltpu.make_async_copy(view, view, self.recv.at[shard, piece]).wait()
+
+    def send_up(self, source, shard, piece):
+        self.send(
+            self.z < self.depth - 1, source, shard, piece, self.up.at[shard, piece], self.head(self.z + 1)
+        )
+
+    def send_down(self, source, shard, piece):
+        self.send(self.z > 0, source, shard, piece, self.down.at[shard, piece], self.head(self.z - 1))
+
+    def send_across(self, cond, source, shard, piece):
+        for j in range(1, self.width):
+            self.send(
+                cond, source, shard, piece, self.cross.at[j - 1, shard, piece], self.head(self.z, j)
+            )
+
+    def start(self):
+        me = self.head(self.z)
+        for piece in range(self.pieces):
+            source = self.own(piece)
+            self.send_across(None, source, me, piece)
+            self.send_up(source, me, piece)
+            self.send_down(source, me, piece)
+
+    def start_early(self):
+        for piece in range(self.early):
+            for j in range(1, self.width):
+                shard = self.head(self.z, j)
+                self.arrive(shard, piece)
+                self.send_up(self.slot(shard, piece), shard, piece)
+                self.send_down(self.slot(shard, piece), shard, piece)
+
+    def sides(self, distance):
+        below, above = self.z - distance, self.z + distance
+        return (
+            (below >= 0, jnp.maximum(below, 0), True),
+            (above < self.depth, jnp.minimum(above, self.depth - 1), False),
+        )
+
+    def stage(self, distance):
+        for piece in range(self.pieces):
+            for there, source_z, upward in self.sides(distance):
+                for j in range(self.width if piece < self.early else 1):
+                    shard = self.head(source_z, j)
+                    view = self.slot(shard, piece)
+                    guarded(there, functools.partial(self.arrive, shard, piece))
+                    if upward and distance < self.depth - 1:
+                        self.send(
+                            there & (self.z < self.depth - 1), view, shard, piece,
+                            self.up.at[shard, piece], self.head(self.z + 1),
+                        )
+                    elif distance < self.depth - 1:
+                        self.send(
+                            there & (self.z > 0), view, shard, piece,
+                            self.down.at[shard, piece], self.head(self.z - 1),
+                        )
+                if piece >= self.early:
+                    shard = self.head(source_z)
+                    self.send_across(there, self.slot(shard, piece), shard, piece)
+
+    def finish(self, shard):
+        for piece in range(self.early, self.pieces):
+            self.arrive(shard, piece)
+
+
+def guarded(cond, action):
+    if cond is None:
+        action()
+    else:
+        pl.when(cond)(action)
+
+
+TOKEN_PIECES, TOKEN_EARLY = 4, 1
+OUT_PIECES, OUT_EARLY = 2, 0
+
+
+def layer_kernel(
+    shards, heads, depth,
+    tokens_ref, beta_ref, wq_ref, wk_ref, wv_ref, gain_ref, wo_ref,
+    out_ref,
+    x_ref, w_ref, raw_ref, wo_all, query_ref, own_ref, states_ref, normed_ref, parts_ref,
+    copy_sems, tok_recv, tok_up, tok_down, tok_cross,
+    wo_recv, wo_up, wo_down, wo_cross, wo_swap_send, wo_swap_recv,
+    state_send, state_recv, part_send, part_recv,
+):
+    ctx, head = lax.axis_index("ctx"), lax.axis_index("head")
+    width = heads // depth
+    rows, features = tokens_ref.shape
+    core, partner = lax.rem(ctx, 2), ctx + 1 - 2 * lax.rem(ctx, 2)
+    pending = []
+
+    loads = [
+        pltpu.make_async_copy(ref, w_ref.at[:, pl.ds(i * DK, DK)], copy_sems.at[i])
+        for i, ref in enumerate((wq_ref, wk_ref, wv_ref))
+    ]
+    loads.append(pltpu.make_async_copy(tokens_ref, x_ref.at[head], copy_sems.at[3]))
+    half = wo_ref.shape[0] // 2
+    loads.append(pltpu.make_async_copy(wo_ref, wo_all.at[head], copy_sems.at[4]))
+    for load in loads:
+        load.start()
+
+    barrier = pltpu.get_barrier_semaphore()
+    for j in range(1, heads):
+        pl.semaphore_signal(
+            barrier, inc=1, device_id={"head": lax.rem(head + j, heads)},
+            device_id_type=pl.DeviceIdType.MESH,
+        )
+    for j in range(1, shards):
+        pl.semaphore_signal(
+            barrier, inc=1, device_id={"ctx": lax.rem(ctx + j, shards)},
+            device_id_type=pl.DeviceIdType.MESH,
+        )
+    pl.semaphore_wait(barrier, heads + shards - 2)
+
+    piece_rows = rows // TOKEN_PIECES
+    gather = LineGather(
+        lambda piece: tokens_ref.at[pl.ds(piece * piece_rows, piece_rows)],
+        lambda shard, piece: x_ref.at[shard, pl.ds(piece * piece_rows, piece_rows)],
+        TOKEN_PIECES, TOKEN_EARLY, depth, width, (tok_recv, tok_up, tok_down, tok_cross), pending,
+    )
+    out_rows = half // OUT_PIECES
+
+    def out_slot(shard, piece):
+        start = pl.multiple_of(core * half + piece * out_rows, 16)
+        return wo_all.at[shard, pl.ds(start, out_rows)]
+
+    def out_own(piece):
+        start = pl.multiple_of(core * half + piece * out_rows, 16)
+        return wo_ref.at[pl.ds(start, out_rows)]
+
+    spread = LineGather(
+        out_own, out_slot, OUT_PIECES, OUT_EARLY, depth, width,
+        (wo_recv, wo_up, wo_down, wo_cross), pending,
+    )
+
+    def swap(shard, cond):
+        start = pl.multiple_of(core * half, 16)
+        view = wo_all.at[shard, pl.ds(start, half)]
+
+        def make():
+            return pltpu.make_async_remote_copy(
+                src_ref=view, dst_ref=view,
+                send_sem=wo_swap_send.at[shard], recv_sem=wo_swap_recv.at[shard],
+                device_id={"ctx": partner}, device_id_type=pl.DeviceIdType.MESH,
+            )
+
+        guarded(cond, lambda: make().start())
+        pending.append((cond, make))
+
+    def spread_stage(distance):
+        if distance < depth:
+            spread.stage(distance)
+            for there, source_z, _ in spread.sides(distance):
+                swap(spread.head(source_z), there)
+        for index, (there, source_z, _) in enumerate(spread.sides(distance - 1)):
+            if distance == 1 and index:
+                continue
+            for j in range(1, width):
+                shard = spread.head(source_z, j)
+                guarded(there, functools.partial(spread.finish, shard))
+                swap(shard, there)
+
+    def project(shard, first=False):
+        tile = 256
+
+        def step(i, carry):
+            span = pl.ds(pl.multiple_of(i * tile, tile), tile)
+            weight = w_ref[pl.ds(pl.multiple_of(shard * features, 128), features), :]
+            term = jnp.dot(x_ref[shard, span, :], weight, preferred_element_type=F32)
+            raw_ref[span, :] = term if first else raw_ref[span, :] + term
+            return carry
+
+        lax.fori_loop(0, rows // tile, step, 0)
+
+    def finish_across(distance):
+        for index, (there, source_z, _) in enumerate(gather.sides(distance)):
+            if distance == 0 and index:
+                continue
+            for j in range(1, width):
+                shard = gather.head(source_z, j)
+
+                def take(shard=shard):
+                    gather.finish(shard)
+                    project(shard)
+
+                guarded(there, take)
+
+    gather.start()
+    for load in loads[:4]:
+        load.wait()
+    gather.start_early()
+    project(head, first=True)
+    for distance in range(1, depth):
+        gather.stage(distance)
+        if distance == depth - 1:
+            spread.start()
+        for there, source_z, _ in gather.sides(distance):
+            guarded(there, functools.partial(project, gather.head(source_z)))
+        finish_across(distance - 1)
+    finish_across(depth - 1)
+    loads[4].wait()
 
     def emit(i, query, own):
-        rows = pl.ds(i * CHUNK, CHUNK)
-        query_ref[rows, :] = query.astype(BF16)
-        own_ref[rows, :] = own
+        span = pl.ds(i * CHUNK, CHUNK)
+        query_ref[span, :] = query.astype(BF16)
+        own_ref[span, :] = own
 
     raw = [
         [raw_ref[pl.ds(i * CHUNK, CHUNK), pl.ds(j * DK, DK)] for j in range(3)]
-        for i in range(count)
+        for i in range(rows // CHUNK)
     ]
-    rates = [beta_ref[pl.ds(i * CHUNK, CHUNK), :] for i in range(count)]
-    state_ref[...] = shard_maps(raw, rates, emit).astype(BF16)
-
-
-def normed_kernel(shards, states_ref, query_ref, own_ref, gain_ref, out_ref):
-    me = lax.axis_index("ctx")
+    rates = [beta_ref[pl.ds(i * CHUNK, CHUNK), :] for i in range(rows // CHUNK)]
+    states_ref[ctx] = shard_maps(raw, rates, emit).astype(BF16)
+
+    for other in range(1, shards):
+        def make(other=other):
+            return pltpu.make_async_remote_copy(
+                src_ref=states_ref.at[ctx], dst_ref=states_ref.at[ctx],
+                send_sem=state_send.at[other], recv_sem=state_recv.at[ctx],
+                device_id={"ctx": jnp.int32(other)}, device_id_type=pl.DeviceIdType.MESH,
+            )
+
+        guarded(ctx < other, lambda make=make: make().start())
+        pending.append((ctx < other, make))
+
+    spread_stage(1)
+    for shard in range(shards - 1):
+        @pl.when(shard < ctx)
+        def _(shard=shard):
+            view = states_ref.at[shard]
+            pltpu.make_async_copy(view, view, state_recv.at[shard]).wait()
+
+        @pl.when(shard >= ctx)
+        def _(shard=shard):
+            @pl.when(shard > ctx)
+            def _():
+                states_ref[shard] = jnp.zeros(states_ref.shape[1:], BF16)
+
     start = jnp.zeros((DK, DK), F32)
     for shard in range(shards - 1):
         state = states_ref[shard]
         after = dot(state[:, :DK], start) + state[:, DK:].astype(F32)
-        start = jnp.where(shard < me, after, start)
-    recurrent = own_ref[...] + dot(query_ref[...], start)
-    scale = lax.rsqrt(jnp.mean(recurrent * recurrent, axis=-1, keepdims=True) + 1e-5)
-    out_ref[...] = (recurrent * scale * gain_ref[...]).astype(BF16)
+        start = jnp.where(shard < ctx, after, start)
+    block = rows // heads
+    for i in range(rows // CHUNK):
+        span = pl.ds(i * CHUNK, CHUNK)
+        recurrent = own_ref[span, :] + dot(query_ref[span, :], start)
+        scale = lax.rsqrt(jnp.mean(recurrent * recurrent, axis=-1, keepdims=True) + 1e-5)
+        normed_ref[span, :] = (recurrent * scale * gain_ref[...]).astype(BF16)
+
+    mine = pl.multiple_of(head * DK, DK)
+    own_part = pltpu.make_async_copy(
+        normed_ref.at[pl.ds(pl.multiple_of(head * block, 16), block)],
+        parts_ref.at[:, pl.ds(mine, DK)], copy_sems.at[5],
+    )
+    own_part.start()
+    for j in range(1, heads):
+        other = lax.rem(head + j, heads)
+
+        def make(other=other, j=j):
+            return pltpu.make_async_remote_copy(
+                src_ref=normed_ref.at[pl.ds(pl.multiple_of(other * block, 16), block)],
+                dst_ref=parts_ref.at[:, pl.ds(mine, DK)],
+                send_sem=part_send.at[j], recv_sem=part_recv.at[j],
+                device_id={"head": other}, device_id_type=pl.DeviceIdType.MESH,
+            )
+
+        make().start()
+        pending.append((None, make))
+
+    for distance in range(2, depth + 1):
+        spread_stage(distance)
+    for j in range(1, heads):
+        source = lax.rem(head + heads - j, heads)
+        view = parts_ref.at[:, pl.ds(pl.multiple_of(source * DK, DK), DK)]
+        pltpu.make_async_copy(view, view, part_recv.at[j]).wait()
+    own_part.wait()
+    other_half = pl.multiple_of((1 - core) * half, 16)
+    for j in range(1, heads):
+        shard = lax.rem(head + j, heads)
+        view = wo_all.at[shard, pl.ds(other_half, half)]
+        pltpu.make_async_copy(view, view, wo_swap_recv.at[shard]).wait()
+
+    tile = 512
+
+    def mix(i, carry):
+        span = pl.ds(pl.multiple_of(i * tile, tile), tile)
+        weight = wo_all[:, :, span].reshape(heads * DK, tile)
+        out_ref[:, span] = jnp.dot(parts_ref[...], weight, preferred_element_type=F32).astype(BF16)
+        return carry
+
+    lax.fori_loop(0, out_ref.shape[1] // tile, mix, 0)
+    for cond, make in pending:
+        guarded(cond, lambda make=make: make().wait_send())
 
 
 def local(tokens, beta, w_query, w_key, w_value, gain, w_out):
-    rows = tokens.shape[0]
+    rows, features = tokens.shape
     shards, heads = lax.axis_size("ctx"), lax.axis_size("head")
-    whole = pl.BlockSpec(memory_space=pltpu.VMEM)
-    portion = lax.all_gather(tokens, "head", axis=1, tiled=True)
-    weights = jnp.concatenate([w_query, w_key, w_value], axis=1)
-    state, query, own = pl.pallas_call(
-        shard_kernel,
-        out_shape=(
-            jax.ShapeDtypeStruct((DK, 2 * DK), BF16),
-            jax.ShapeDtypeStruct((rows, DK), BF16),
-            jax.ShapeDtypeStruct((rows, DK), F32),
+    depth = 4 if heads % 4 == 0 else 1
+    width = heads // depth
+    model = w_query.shape[0]
+    vmem, hbm = pl.BlockSpec(memory_space=pltpu.VMEM), pl.BlockSpec(memory_space=pl.ANY)
+    dma = pltpu.SemaphoreType.DMA
+    return pl.pallas_call(
+        functools.partial(layer_kernel, shards, heads, depth),
+        out_shape=jax.ShapeDtypeStruct((rows // heads, w_out.shape[1]), BF16),
+        in_specs=[hbm, vmem, hbm, hbm, hbm, vmem, hbm],
+        out_specs=vmem,
+        scratch_shapes=[
+            pltpu.VMEM((heads, rows, features), BF16),
+            pltpu.VMEM((model, 3 * DK), BF16),
+            pltpu.VMEM((rows, 3 * DK), F32),
+            pltpu.VMEM((heads, DK, w_out.shape[1]), BF16),
+            pltpu.VMEM((rows, DK), BF16),
+            pltpu.VMEM((rows, DK), F32),
+            pltpu.VMEM((shards, DK, 2 * DK), BF16),
+            pltpu.VMEM((rows, DK), BF16),
+            pltpu.VMEM((rows // heads, heads * DK), BF16),
+            dma((6,)),
+            dma((heads, TOKEN_PIECES)),
+            dma((heads, TOKEN_PIECES)),
+            dma((heads, TOKEN_PIECES)),
+            dma((width - 1, heads, TOKEN_PIECES)),
+            dma((heads, OUT_PIECES)),
+            dma((heads, OUT_PIECES)),
+            dma((heads, OUT_PIECES)),
+            dma((width - 1, heads, OUT_PIECES)),
+            dma((heads,)),
+            dma((heads,)),
+            dma((shards,)),
+            dma((shards,)),
+            dma((heads,)),
+            dma((heads,)),
+        ],
+        compiler_params=pltpu.CompilerParams(
+            collective_id=0, has_side_effects=True, vmem_limit_bytes=48 * 2**20
         ),
-        in_specs=[whole] * 3,
-        out_specs=(whole,) * 3,
-        scratch_shapes=[pltpu.VMEM((rows, 3 * DK), F32)],
-        compiler_params=pltpu.CompilerParams(vmem_limit_bytes=40 * 2**20),
-    )(portion, weights, beta)
-    states = lax.all_gather(state, "ctx")
-    normed = pl.pallas_call(
-        functools.partial(normed_kernel, shards),
-        out_shape=jax.ShapeDtypeStruct((rows, DK), BF16),
-        in_specs=[whole] * 4,
-        out_specs=whole,
-        compiler_params=pltpu.CompilerParams(vmem_limit_bytes=20 * 2**20),
-    )(states, query, own, gain.reshape(1, DK))
-    parts = lax.all_to_all(normed.reshape(heads, rows // heads, DK), "head", 0, 0)
-    w_all = lax.all_gather(w_out, "head", axis=0, tiled=True)
-    mixed_rows = parts.transpose(1, 0, 2).reshape(rows // heads, heads * DK)
-    return jnp.dot(mixed_rows, w_all, preferred_element_type=F32).astype(BF16)
+    )(tokens, beta, w_query, w_key, w_value, gain.reshape(1, DK), w_out)
 
 
 def solution(mesh):

time: 177 us -> 91.9 us (0.52)
  waiting for transfers between devices: 137 us -> 0 us
  Pallas kernels: 8.03 us -> 84.5 us
  between operations: 13.4 us -> 0.02 us
  blocking collectives: 5.79 us -> 0 us
  matrix products: 3.73 us -> 0 us
  starting transfers between devices: 3.45 us -> 0 us
  local copies, waits for them, and re-layouts: 3.94 us -> 6.01 us
    all_gather x2 -> x0, waiting for transfers between devices: 136 us -> none  [the longest x1 76.7 us: local(): portion = lax.all_gather(tokens, 'head', axis=1, tiled=True)]
    pallas_call x2 -> x1, Pallas kernels: 8.03 us -> 84.5 us  [local(): pl.pallas_call(functools.partial(layer_kernel, shards, heads, depth), out...]
    all_gather x1 -> x0, blocking collectives: 5.79 us -> none  [local(): states = lax.all_gather(state, 'ctx')]
    dot_general x1 -> x0, matrix products: 3.73 us -> none  [local(): return jnp.dot(mixed_rows, w_all, preferred_element_type=F32).astype(BF16)]
    all_to_all x1 -> x0, starting transfers between devices: 3.41 us -> none  [local(): lax.all_to_all(normed.reshape(heads, rows // heads, DK), 'head', 0, 0)]
    unnamed x5 -> x14, local copies, waits for them, and re-layouts: 3.09 us -> 6.01 us
  transfers between devices with their start and end apart: 3 -> 0, of which waited for: 2 -> 0; matrix products, arithmetic and copies ran while one was open for 2% -> 0% of each run, Pallas kernels for 5% -> 0%
where the time goes in v2:
time: 91.9 us; the launch traced here: 90.5 us
  Pallas kernels  84.5 us (92%)
  local copies, waits for them, and re-layouts  6.01 us (7%)
    pallas_call x1, Pallas kernels, local(): pl.pallas_call(functools.partial(layer_kernel, shards, heads, depth), out...  84.5 us
    unnamed x14, local copies, waits for them, and re-layouts  6.01 us

profile of v2, /device:TPU:0, one launch (start us, length us, event | category | flops | bytes accessed | tf_op | source)
XLA Modules:
  0.0 90.5 jit_solution(13762087551409480968)
XLA Ops:
  0.0 0.0 copy-start
  0.0 0.0 copy-start.5
  0.0 1.0 %copy.8.beta_ref = f32[1024,1]{1,0:T(8,128)S(1)} copy(f32[1024,1]{0,1:T(1,128)} %param.8) | data formatting | bytes 8192 | tf_op args[1]
  1.0 0.1 copy-done
  1.1 0.0 copy-done.5
  1.1 0.0 copy-start.1
  1.1 1.0 %copy-done.1 = bf16[2048,128]{1,0:T(8,128)(2,1)S(1)} copy-done((bf16[2048,128]{1,0:T(8,128)(2,1)S(1)}, bf16[2048,128]{1,0:T(8,128)(2,1)}, u32[]{:S(2)}) %copy-start.1) | copy-done | bytes 524312
  2.1 0.0 copy-start.2
  2.1 1.0 %copy-done.2 = bf16[2048,128]{1,0:T(8,128)(2,1)S(1)} copy-done((bf16[2048,128]{1,0:T(8,128)(2,1)S(1)}, bf16[2048,128]{1,0:T(8,128)(2,1)}, u32[]{:S(2)}) %copy-start.2) | copy-done | bytes 524312
  3.1 0.0 copy-start.3
  3.1 1.0 %copy-done.3 = bf16[2048,128]{1,0:T(8,128)(2,1)S(1)} copy-done((bf16[2048,128]{1,0:T(8,128)(2,1)S(1)}, bf16[2048,128]{1,0:T(8,128)(2,1)}, u32[]{:S(2)}) %copy-start.3) | copy-done | bytes 524312
  4.2 0.0 copy-start.4
  4.2 1.0 %copy-done.4 = bf16[128,2048]{1,0:T(8,128)(2,1)S(1)} copy-done((bf16[128,2048]{1,0:T(8,128)(2,1)S(1)}, bf16[128,2048]{1,0:T(8,128)(2,1)}, u32[]{:S(2)}) %copy-start.4) | copy-done | bytes 524312
  5.2 84.5 %shard_map.73 = bf16[128,2048]{1,0:T(8,128)(2,1)S(1)} custom-call(bf16[1024,256]{1,0:T(8,128)(2,1)S(1)} %copy-done, f32[1024,1]{1,0:T(8,128)S(1)} %copy.8.beta_ref, bf16[2048,128]{1,0:T(8,128)(2,1)S(1)} %copy-done.1, bf16[2048,128]{1,0:T(8,128)(2,1)S(1)} %copy-done.2, bf16[2048,128]{1,0:T(8,128)(2,1)S(1)} %copy-done.3, f32[1,128]{1,0:T(1,128)S(1)} %bitcast.1, ...), custom_call_target="tpu_custom_call" | custom-call | tf_op jit(solution)/shard_map/pallas_call | solution.py:425
  89.7 0.8 copy.10
Async XLA Ops:
  0.0 1.1 %copy-start = (bf16[1024,256]{1,0:T(8,128)(2,1)S(1)}, bf16[1024,256]{1,0:T(8,128)(2,1)}, u32[]{:S(2)}) copy-start(bf16[1024,256]{1,0:T(8,128)(2,1)} %tokens_ref.1) | copy-start | bytes 1572868
  0.0 1.1 %copy-start.5 = (f32[128]{0:T(128)S(1)}, f32[128]{0:T(128)}, u32[]{:S(2)}) copy-start(f32[128]{0:T(128)} %param.12) | copy-start | bytes 1540
  1.1 1.0 %copy-start.1 = (bf16[2048,128]{1,0:T(8,128)(2,1)S(1)}, bf16[2048,128]{1,0:T(8,128)(2,1)}, u32[]{:S(2)}) copy-start(bf16[2048,128]{1,0:T(8,128)(2,1)} %wq_ref.1) | copy-start | bytes 1572868
  2.1 1.0 %copy-start.2 = (bf16[2048,128]{1,0:T(8,128)(2,1)S(1)}, bf16[2048,128]{1,0:T(8,128)(2,1)}, u32[]{:S(2)}) copy-start(bf16[2048,128]{1,0:T(8,128)(2,1)} %wk_ref.1) | copy-start | bytes 1572868
  3.1 1.0 %copy-start.3 = (bf16[2048,128]{1,0:T(8,128)(2,1)S(1)}, bf16[2048,128]{1,0:T(8,128)(2,1)}, u32[]{:S(2)}) copy-start(bf16[2048,128]{1,0:T(8,128)(2,1)} %wv_ref.1) | copy-start | bytes 1572868
  4.2 1.0 %copy-start.4 = (bf16[128,2048]{1,0:T(8,128)(2,1)S(1)}, bf16[128,2048]{1,0:T(8,128)(2,1)}, u32[]{:S(2)}) copy-start(bf16[128,2048]{1,0:T(8,128)(2,1)} %wo_ref.1) | copy-start | bytes 1572868

commit v3 on v2

--- a/solution.py
+++ b/solution.py
@@ -58,7 +58,7 @@
     return inverses
 
 
-def shard_maps(raw, rates, emit):
+def shard_maps(raw, rates, emit, midway):
     count = len(raw)
     row = lax.broadcasted_iota(jnp.int32, (CHUNK, CHUNK), 0)
     col = lax.broadcasted_iota(jnp.int32, (CHUNK, CHUNK), 1)
@@ -68,6 +68,7 @@
         jnp.where(row > col, rates[i] * dot_nt(keys[i], keys[i]), 0.0) for i in range(count)
     ]
     inverses = unit_lower_inverses(lowers)
+    midway()
     factors = [
         dot(inverses[i], jnp.concatenate([rates[i] * keys[i], rates[i] * raw[i][2]], axis=1))
         for i in range(count)
@@ -268,12 +269,13 @@
         pending.append((cond, make))
 
     def spread_stage(distance):
-        if distance < depth:
-            spread.stage(distance)
-            for there, source_z, _ in spread.sides(distance):
-                swap(spread.head(source_z), there)
-        for index, (there, source_z, _) in enumerate(spread.sides(distance - 1)):
-            if distance == 1 and index:
+        spread.stage(distance)
+        for there, source_z, _ in spread.sides(distance):
+            swap(spread.head(source_z), there)
+
+    def spread_across(distance):
+        for index, (there, source_z, _) in enumerate(spread.sides(distance)):
+            if distance == 0 and index:
                 continue
             for j in range(1, width):
                 shard = spread.head(source_z, j)
@@ -312,8 +314,10 @@
     project(head, first=True)
     for distance in range(1, depth):
         gather.stage(distance)
+        if distance == 1:
+            spread.start()
         if distance == depth - 1:
-            spread.start()
+            spread_stage(1)
         for there, source_z, _ in gather.sides(distance):
             guarded(there, functools.partial(project, gather.head(source_z)))
         finish_across(distance - 1)
@@ -329,8 +333,9 @@
         [raw_ref[pl.ds(i * CHUNK, CHUNK), pl.ds(j * DK, DK)] for j in range(3)]
         for i in range(rows // CHUNK)
     ]
-    rates = [beta_ref[pl.ds(i * CHUNK, CHUNK), :] for i in range(rows // CHUNK)]
-    states_ref[ctx] = shard_maps(raw, rates, emit).astype(BF16)
+    rate_columns = beta_ref[...].T
+    rates = [rate_columns[:, i : i + 1] for i in range(rows // CHUNK)]
+    states_ref[ctx] = shard_maps(raw, rates, emit, functools.partial(spread_stage, 2)).astype(BF16)
 
     for other in range(1, shards):
         def make(other=other):
@@ -343,7 +348,7 @@
         guarded(ctx < other, lambda make=make: make().start())
         pending.append((ctx < other, make))
 
-    spread_stage(1)
+    spread_stage(3)
     for shard in range(shards - 1):
         @pl.when(shard < ctx)
         def _(shard=shard):
@@ -388,8 +393,8 @@
         make().start()
         pending.append((None, make))
 
-    for distance in range(2, depth + 1):
-        spread_stage(distance)
+    for distance in range(depth):
+        spread_across(distance)
     for j in range(1, heads):
         source = lax.rem(head + heads - j, heads)
         view = parts_ref.at[:, pl.ds(pl.multiple_of(source * DK, DK), DK)]
@@ -417,7 +422,7 @@
 def local(tokens, beta, w_query, w_key, w_value, gain, w_out):
     rows, features = tokens.shape
     shards, heads = lax.axis_size("ctx"), lax.axis_size("head")
-    depth = 4 if heads % 4 == 0 else 1
+    depth = 4
     width = heads // depth
     model = w_query.shape[0]
     vmem, hbm = pl.BlockSpec(memory_space=pltpu.VMEM), pl.BlockSpec(memory_space=pl.ANY)
@@ -454,9 +459,9 @@
             dma((heads,)),
         ],
         compiler_params=pltpu.CompilerParams(
-            collective_id=0, has_side_effects=True, vmem_limit_bytes=48 * 2**20
+            collective_id=0, has_side_effects=True, vmem_limit_bytes=60 * 2**20
         ),
-    )(tokens, beta, w_query, w_key, w_value, gain.reshape(1, DK), w_out)
+    )(tokens, beta.reshape(rows // CHUNK, CHUNK), w_query, w_key, w_value, gain.reshape(1, DK), w_out)
 
 
 def solution(mesh):

time: 91.9 us -> 87.6 us (0.953)
  local copies, waits for them, and re-layouts: 6.01 us -> 1.88 us
    unnamed x14 -> x1, local copies, waits for them, and re-layouts: 6.01 us -> 1.88 us
where the time goes in v3:
time: 87.6 us; the launch traced here: 86.7 us
  Pallas kernels  84.9 us (97%)
  local copies, waits for them, and re-layouts  1.88 us (2%)
    pallas_call x1, Pallas kernels, local(): pl.pallas_call(functools.partial(layer_kernel, shards, heads, depth), out...  84.9 us
    unnamed x1, local copies, waits for them, and re-layouts  1.88 us

profile of v3, /device:TPU:0, one launch (start us, length us, event | category | flops | bytes accessed | tf_op | source)
XLA Modules:
  0.0 86.7 jit_solution(8658481289325680922)
XLA Ops:
  0.0 84.9 %shard_map.73 = bf16[128,2048]{1,0:T(8,128)(2,1)} custom-call(bf16[1024,256]{1,0:T(8,128)(2,1)} %tokens_ref.1, f32[8,128]{1,0:T(8,128)} %bitcast.2, bf16[2048,128]{1,0:T(8,128)(2,1)} %wq_ref.1, bf16[2048,128]{1,0:T(8,128)(2,1)} %wk_ref.1, bf16[2048,128]{1,0:T(8,128)(2,1)} %wv_ref.1, f32[1,128]{1,0:T(1,128)} %bitcast.3, bf16[128,2048]{1,0:T(8,128)(2,1)} %wo_ref.1), custom_call_target="tpu_custom_call" | custom-call | tf_op jit(solution)/shard_map/pallas_call | solution.py:430
  84.9 1.9 %copy.9 = bf16[128,2048]{1,0:T(8,128)(2,1)} copy(bf16[128,2048]{1,0:T(8,128)(2,1)} %shard_map.73) | data formatting | bytes 1048576

commit v4 on v3

--- a/solution.py
+++ b/solution.py
@@ -192,7 +192,7 @@
 
 
 TOKEN_PIECES, TOKEN_EARLY = 4, 1
-OUT_PIECES, OUT_EARLY = 2, 0
+OUT_PIECES, OUT_EARLY = 1, 0
 
 
 def layer_kernel(
@@ -201,13 +201,14 @@
     out_ref,
     x_ref, w_ref, raw_ref, wo_all, query_ref, own_ref, states_ref, normed_ref, parts_ref,
     copy_sems, tok_recv, tok_up, tok_down, tok_cross,
-    wo_recv, wo_up, wo_down, wo_cross, wo_swap_send, wo_swap_recv,
+    wo_recv, wo_up, wo_down, wo_cross, core_send, core_recv, pair_send, pair_recv,
     state_send, state_recv, part_send, part_recv,
 ):
     ctx, head = lax.axis_index("ctx"), lax.axis_index("head")
     width = heads // depth
     rows, features = tokens_ref.shape
-    core, partner = lax.rem(ctx, 2), ctx + 1 - 2 * lax.rem(ctx, 2)
+    core, pair = lax.rem(ctx, 2), lax.rem(ctx // 2, 2)
+    core_partner, pair_partner = ctx + 1 - 2 * core, ctx + 2 - 4 * pair
     pending = []
 
     loads = [
@@ -215,7 +216,7 @@
         for i, ref in enumerate((wq_ref, wk_ref, wv_ref))
     ]
     loads.append(pltpu.make_async_copy(tokens_ref, x_ref.at[head], copy_sems.at[3]))
-    half = wo_ref.shape[0] // 2
+    quarter = wo_ref.shape[0] // 4
     loads.append(pltpu.make_async_copy(wo_ref, wo_all.at[head], copy_sems.at[4]))
     for load in loads:
         load.start()
@@ -239,34 +240,46 @@
         lambda shard, piece: x_ref.at[shard, pl.ds(piece * piece_rows, piece_rows)],
         TOKEN_PIECES, TOKEN_EARLY, depth, width, (tok_recv, tok_up, tok_down, tok_cross), pending,
     )
-    out_rows = half // OUT_PIECES
+    out_rows = quarter // OUT_PIECES
+
+    def quarter_start(pair, core):
+        return (2 * pair + core) * quarter
 
     def out_slot(shard, piece):
-        start = pl.multiple_of(core * half + piece * out_rows, 16)
+        start = pl.multiple_of(quarter_start(pair, core) + piece * out_rows, 16)
         return wo_all.at[shard, pl.ds(start, out_rows)]
 
     def out_own(piece):
-        start = pl.multiple_of(core * half + piece * out_rows, 16)
+        start = pl.multiple_of(quarter_start(pair, core) + piece * out_rows, 16)
         return wo_ref.at[pl.ds(start, out_rows)]
+
+    def out_quarter(shard, pair, core):
+        return wo_all.at[shard, pl.ds(pl.multiple_of(quarter_start(pair, core), 16), quarter)]
 
     spread = LineGather(
         out_own, out_slot, OUT_PIECES, OUT_EARLY, depth, width,
         (wo_recv, wo_up, wo_down, wo_cross), pending,
     )
 
-    def swap(shard, cond):
-        start = pl.multiple_of(core * half, 16)
-        view = wo_all.at[shard, pl.ds(start, half)]
-
+    def hand_over(cond, view, send_sem, recv_sem, target):
         def make():
             return pltpu.make_async_remote_copy(
-                src_ref=view, dst_ref=view,
-                send_sem=wo_swap_send.at[shard], recv_sem=wo_swap_recv.at[shard],
-                device_id={"ctx": partner}, device_id_type=pl.DeviceIdType.MESH,
+                src_ref=view, dst_ref=view, send_sem=send_sem, recv_sem=recv_sem,
+                device_id={"ctx": target}, device_id_type=pl.DeviceIdType.MESH,
             )
 
         guarded(cond, lambda: make().start())
         pending.append((cond, make))
+
+    def swap(shard, cond):
+        view = out_quarter(shard, pair, core)
+        hand_over(cond, view, pair_send.at[shard], pair_recv.at[shard], pair_partner)
+        hand_over(cond, view, core_send.at[shard, 0], core_recv.at[shard, 0], core_partner)
+
+    def swap_paired(shard, cond):
+        view = out_quarter(shard, 1 - pair, core)
+        guarded(cond, pltpu.make_async_copy(view, view, pair_recv.at[shard]).wait)
+        hand_over(cond, view, core_send.at[shard, 1], core_recv.at[shard, 1], core_partner)
 
     def spread_stage(distance):
         spread.stage(distance)
@@ -314,15 +327,18 @@
     project(head, first=True)
     for distance in range(1, depth):
         gather.stage(distance)
-        if distance == 1:
+        if distance == 2:
             spread.start()
-        if distance == depth - 1:
-            spread_stage(1)
         for there, source_z, _ in gather.sides(distance):
             guarded(there, functools.partial(project, gather.head(source_z)))
         finish_across(distance - 1)
+    spread_stage(1)
     finish_across(depth - 1)
     loads[4].wait()
+
+    def midway():
+        spread_across(0)
+        spread_stage(2)
 
     def emit(i, query, own):
         span = pl.ds(i * CHUNK, CHUNK)
@@ -335,7 +351,7 @@
     ]
     rate_columns = beta_ref[...].T
     rates = [rate_columns[:, i : i + 1] for i in range(rows // CHUNK)]
-    states_ref[ctx] = shard_maps(raw, rates, emit, functools.partial(spread_stage, 2)).astype(BF16)
+    states_ref[ctx] = shard_maps(raw, rates, emit, midway).astype(BF16)
 
     for other in range(1, shards):
         def make(other=other):
@@ -393,18 +409,24 @@
         make().start()
         pending.append((None, make))
 
+    for distance in range(1, depth):
+        spread_across(distance)
     for distance in range(depth):
-        spread_across(distance)
+        for index, (there, source_z, _) in enumerate(spread.sides(distance)):
+            if distance == 0 and index:
+                continue
+            for j in range(0 if distance else 1, width):
+                swap_paired(spread.head(source_z, j), there)
     for j in range(1, heads):
         source = lax.rem(head + heads - j, heads)
         view = parts_ref.at[:, pl.ds(pl.multiple_of(source * DK, DK), DK)]
         pltpu.make_async_copy(view, view, part_recv.at[j]).wait()
     own_part.wait()
-    other_half = pl.multiple_of((1 - core) * half, 16)
     for j in range(1, heads):
         shard = lax.rem(head + j, heads)
-        view = wo_all.at[shard, pl.ds(other_half, half)]
-        pltpu.make_async_copy(view, view, wo_swap_recv.at[shard]).wait()
+        for index, from_pair in enumerate((pair, 1 - pair)):
+            view = out_quarter(shard, from_pair, 1 - core)
+            pltpu.make_async_copy(view, view, core_recv.at[shard, index]).wait()
 
     tile = 512
 
@@ -451,6 +473,8 @@
             dma((heads, OUT_PIECES)),
             dma((heads, OUT_PIECES)),
             dma((width - 1, heads, OUT_PIECES)),
+            dma((heads, 2)),
+            dma((heads, 2)),
             dma((heads,)),
             dma((heads,)),
             dma((shards,)),

time: 87.6 us -> 88.3 us (level)
  Pallas kernels: 84.9 us -> 86.2 us
    pallas_call x1, Pallas kernels: 84.9 us -> 86.2 us  [local(): pl.pallas_call(functools.partial(layer_kernel, shards, heads, depth), out...]
where the time goes in v4:
time: 88.3 us; the launch traced here: 88.1 us
  Pallas kernels  86.2 us (98%)
  local copies, waits for them, and re-layouts  1.88 us (2%)
    pallas_call x1, Pallas kernels, local(): pl.pallas_call(functools.partial(layer_kernel, shards, heads, depth), out...  86.2 us
    unnamed x1, local copies, waits for them, and re-layouts  1.88 us

profile of v4, /device:TPU:0, one launch (start us, length us, event | category | flops | bytes accessed | tf_op | source)
XLA Modules:
  0.0 88.1 jit_solution(9374774286254471270)
XLA Ops:
  0.0 86.2 %shard_map.73 = bf16[128,2048]{1,0:T(8,128)(2,1)} custom-call(bf16[1024,256]{1,0:T(8,128)(2,1)} %tokens_ref.1, f32[8,128]{1,0:T(8,128)} %bitcast.2, bf16[2048,128]{1,0:T(8,128)(2,1)} %wq_ref.1, bf16[2048,128]{1,0:T(8,128)(2,1)} %wk_ref.1, bf16[2048,128]{1,0:T(8,128)(2,1)} %wv_ref.1, f32[1,128]{1,0:T(1,128)} %bitcast.3, bf16[128,2048]{1,0:T(8,128)(2,1)} %wo_ref.1), custom_call_target="tpu_custom_call" | custom-call | tf_op jit(solution)/shard_map/pallas_call | solution.py:452
  86.2 1.9 %copy.9 = bf16[128,2048]{1,0:T(8,128)(2,1)} copy(bf16[128,2048]{1,0:T(8,128)(2,1)} %shard_map.73) | data formatting | bytes 1048576

commit v5 on v4

--- a/solution.py
+++ b/solution.py
@@ -191,7 +191,7 @@
         pl.when(cond)(action)
 
 
-TOKEN_PIECES, TOKEN_EARLY = 4, 1
+TOKEN_PIECES, TOKEN_EARLY = 4, 0
 OUT_PIECES, OUT_EARLY = 1, 0
 
 

time: 88.3 us -> 88.4 us (level)
  no operation moved by 1% of the time
where the time goes in v5:
time: 88.4 us; the launch traced here: 88.2 us
  Pallas kernels  86.3 us (98%)
  local copies, waits for them, and re-layouts  1.88 us (2%)
    pallas_call x1, Pallas kernels, local(): pl.pallas_call(functools.partial(layer_kernel, shards, heads, depth), out...  86.3 us
    unnamed x1, local copies, waits for them, and re-layouts  1.88 us

profile of v5, /device:TPU:0, one launch (start us, length us, event | category | flops | bytes accessed | tf_op | source)
XLA Modules:
  0.0 88.2 jit_solution(6888411657896190566)
XLA Ops:
  0.0 86.3 %shard_map.73 = bf16[128,2048]{1,0:T(8,128)(2,1)} custom-call(bf16[1024,256]{1,0:T(8,128)(2,1)} %tokens_ref.1, f32[8,128]{1,0:T(8,128)} %bitcast.2, bf16[2048,128]{1,0:T(8,128)(2,1)} %wq_ref.1, bf16[2048,128]{1,0:T(8,128)(2,1)} %wk_ref.1, bf16[2048,128]{1,0:T(8,128)(2,1)} %wv_ref.1, f32[1,128]{1,0:T(1,128)} %bitcast.3, bf16[128,2048]{1,0:T(8,128)(2,1)} %wo_ref.1), custom_call_target="tpu_custom_call" | custom-call | tf_op jit(solution)/shard_map/pallas_call | solution.py:452
  86.3 1.9 %copy.9 = bf16[128,2048]{1,0:T(8,128)(2,1)} copy(bf16[128,2048]{1,0:T(8,128)(2,1)} %shard_map.73) | data formatting | bytes 1048576

commit v6 on v5

--- a/solution.py
+++ b/solution.py
@@ -192,7 +192,7 @@
 
 
 TOKEN_PIECES, TOKEN_EARLY = 4, 0
-OUT_PIECES, OUT_EARLY = 1, 0
+OUT_PIECES, OUT_EARLY = 1, 1
 
 
 def layer_kernel(
@@ -281,19 +281,12 @@
         guarded(cond, pltpu.make_async_copy(view, view, pair_recv.at[shard]).wait)
         hand_over(cond, view, core_send.at[shard, 1], core_recv.at[shard, 1], core_partner)
 
-    def spread_stage(distance):
-        spread.stage(distance)
-        for there, source_z, _ in spread.sides(distance):
-            swap(spread.head(source_z), there)
-
-    def spread_across(distance):
+    def at_distance(distance, action):
         for index, (there, source_z, _) in enumerate(spread.sides(distance)):
             if distance == 0 and index:
                 continue
-            for j in range(1, width):
-                shard = spread.head(source_z, j)
-                guarded(there, functools.partial(spread.finish, shard))
-                swap(shard, there)
+            for j in range(0 if distance else 1, width):
+                action(spread.head(source_z, j), there)
 
     def project(shard, first=False):
         tile = 256
@@ -320,25 +313,27 @@
 
                 guarded(there, take)
 
+    spread.start()
     gather.start()
     for load in loads[:4]:
         load.wait()
+    spread.start_early()
+    at_distance(0, swap)
     gather.start_early()
     project(head, first=True)
     for distance in range(1, depth):
         gather.stage(distance)
-        if distance == 2:
-            spread.start()
+        spread.stage(distance)
+        at_distance(distance, swap)
+        at_distance(distance - 1, swap_paired)
         for there, source_z, _ in gather.sides(distance):
             guarded(there, functools.partial(project, gather.head(source_z)))
         finish_across(distance - 1)
-    spread_stage(1)
     finish_across(depth - 1)
     loads[4].wait()
 
     def midway():
-        spread_across(0)
-        spread_stage(2)
+        at_distance(depth - 1, swap_paired)
 
     def emit(i, query, own):
         span = pl.ds(i * CHUNK, CHUNK)
@@ -364,7 +359,6 @@
         guarded(ctx < other, lambda make=make: make().start())
         pending.append((ctx < other, make))
 
-    spread_stage(3)
     for shard in range(shards - 1):
         @pl.when(shard < ctx)
         def _(shard=shard):
@@ -409,14 +403,6 @@
         make().start()
         pending.append((None, make))
 
-    for distance in range(1, depth):
-        spread_across(distance)
-    for distance in range(depth):
-        for index, (there, source_z, _) in enumerate(spread.sides(distance)):
-            if distance == 0 and index:
-                continue
-            for j in range(0 if distance else 1, width):
-                swap_paired(spread.head(source_z, j), there)
     for j in range(1, heads):
         source = lax.rem(head + heads - j, heads)
         view = parts_ref.at[:, pl.ds(pl.multiple_of(source * DK, DK), DK)]

time: 88.4 us -> 81.8 us (0.925)
  the two profiles are of different devices: /device:TPU:0 before, /device:TPU:31 now
where the time goes in v6:
time: 81.8 us; the launch traced here: 81.6 us
  Pallas kernels  79.7 us (97%)
  local copies, waits for them, and re-layouts  1.88 us (2%)
    pallas_call x1, Pallas kernels, local(): pl.pallas_call(functools.partial(layer_kernel, shards, heads, depth), out...  79.7 us
    unnamed x1, local copies, waits for them, and re-layouts  1.88 us

profile of v6, /device:TPU:31, one launch (start us, length us, event | category | flops | bytes accessed | tf_op | source)
XLA Modules:
  0.0 81.6 jit_solution(5041489038772045508)
XLA Ops:
  0.0 79.7 %shard_map.73 = bf16[128,2048]{1,0:T(8,128)(2,1)} custom-call(bf16[1024,256]{1,0:T(8,128)(2,1)} %tokens_ref.1, f32[8,128]{1,0:T(8,128)} %bitcast.2, bf16[2048,128]{1,0:T(8,128)(2,1)} %wq_ref.1, bf16[2048,128]{1,0:T(8,128)(2,1)} %wk_ref.1, bf16[2048,128]{1,0:T(8,128)(2,1)} %wv_ref.1, f32[1,128]{1,0:T(1,128)} %bitcast.3, bf16[128,2048]{1,0:T(8,128)(2,1)} %wo_ref.1), custom_call_target="tpu_custom_call" | custom-call | tf_op jit(solution)/shard_map/pallas_call | solution.py:438
  79.7 1.9 %copy.9 = bf16[128,2048]{1,0:T(8,128)(2,1)} copy(bf16[128,2048]{1,0:T(8,128)(2,1)} %shard_map.73) | data formatting | bytes 1048576

commit v7 on v6

--- a/solution.py
+++ b/solution.py
@@ -191,7 +191,7 @@
         pl.when(cond)(action)
 
 
-TOKEN_PIECES, TOKEN_EARLY = 4, 0
+TOKEN_PIECES, TOKEN_EARLY = 8, 0
 OUT_PIECES, OUT_EARLY = 1, 1
 
 

time: 81.8 us -> 83 us (1.015)
  Pallas kernels: 79.7 us -> 80.9 us
    pallas_call x1, Pallas kernels: 79.7 us -> 80.9 us  [local(): pl.pallas_call(functools.partial(layer_kernel, shards, heads, depth), out...]
where the time goes in v7:
time: 83 us; the launch traced here: 82.8 us
  Pallas kernels  80.9 us (97%)
  local copies, waits for them, and re-layouts  1.88 us (2%)
    pallas_call x1, Pallas kernels, local(): pl.pallas_call(functools.partial(layer_kernel, shards, heads, depth), out...  80.9 us
    unnamed x1, local copies, waits for them, and re-layouts  1.88 us

profile of v7, /device:TPU:31, one launch (start us, length us, event | category | flops | bytes accessed | tf_op | source)
XLA Modules:
  0.0 82.8 jit_solution(6479777667698099165)
XLA Ops:
  0.0 80.9 %shard_map.73 = bf16[128,2048]{1,0:T(8,128)(2,1)} custom-call(bf16[1024,256]{1,0:T(8,128)(2,1)} %tokens_ref.1, f32[8,128]{1,0:T(8,128)} %bitcast.2, bf16[2048,128]{1,0:T(8,128)(2,1)} %wq_ref.1, bf16[2048,128]{1,0:T(8,128)(2,1)} %wk_ref.1, bf16[2048,128]{1,0:T(8,128)(2,1)} %wv_ref.1, f32[1,128]{1,0:T(1,128)} %bitcast.3, bf16[128,2048]{1,0:T(8,128)(2,1)} %wo_ref.1), custom_call_target="tpu_custom_call" | custom-call | tf_op jit(solution)/shard_map/pallas_call | solution.py:438
  80.9 1.9 %copy.9 = bf16[128,2048]{1,0:T(8,128)(2,1)} copy(bf16[128,2048]{1,0:T(8,128)(2,1)} %shard_map.73) | data formatting | bytes 1048576

commit v8 on v6

--- a/solution.py
+++ b/solution.py
@@ -323,9 +323,10 @@
     project(head, first=True)
     for distance in range(1, depth):
         gather.stage(distance)
-        spread.stage(distance)
-        at_distance(distance, swap)
-        at_distance(distance - 1, swap_paired)
+        if distance > 1:
+            spread.stage(distance - 1)
+            at_distance(distance - 1, swap)
+            at_distance(distance - 2, swap_paired)
         for there, source_z, _ in gather.sides(distance):
             guarded(there, functools.partial(project, gather.head(source_z)))
         finish_across(distance - 1)
@@ -333,7 +334,9 @@
     loads[4].wait()
 
     def midway():
-        at_distance(depth - 1, swap_paired)
+        spread.stage(depth - 1)
+        at_distance(depth - 1, swap)
+        at_distance(depth - 2, swap_paired)
 
     def emit(i, query, own):
         span = pl.ds(i * CHUNK, CHUNK)
@@ -403,6 +406,7 @@
         make().start()
         pending.append((None, make))
 
+    at_distance(depth - 1, swap_paired)
     for j in range(1, heads):
         source = lax.rem(head + heads - j, heads)
         view = parts_ref.at[:, pl.ds(pl.multiple_of(source * DK, DK), DK)]

time: 81.8 us -> 79.2 us (0.968)
  the two profiles are of different devices: /device:TPU:31 before, /device:TPU:23 now
where the time goes in v8:
time: 79.2 us; the launch traced here: 79 us
  Pallas kernels  77.1 us (97%)
  local copies, waits for them, and re-layouts  1.88 us (2%)
    pallas_call x1, Pallas kernels, local(): pl.pallas_call(functools.partial(layer_kernel, shards, heads, depth), out...  77.1 us
    unnamed x1, local copies, waits for them, and re-layouts  1.88 us

profile of v8, /device:TPU:23, one launch (start us, length us, event | category | flops | bytes accessed | tf_op | source)
XLA Modules:
  0.0 79.0 jit_solution(8889891217530833886)
XLA Ops:
  0.0 77.1 %shard_map.73 = bf16[128,2048]{1,0:T(8,128)(2,1)} custom-call(bf16[1024,256]{1,0:T(8,128)(2,1)} %tokens_ref.1, f32[8,128]{1,0:T(8,128)} %bitcast.2, bf16[2048,128]{1,0:T(8,128)(2,1)} %wq_ref.1, bf16[2048,128]{1,0:T(8,128)(2,1)} %wk_ref.1, bf16[2048,128]{1,0:T(8,128)(2,1)} %wv_ref.1, f32[1,128]{1,0:T(1,128)} %bitcast.3, bf16[128,2048]{1,0:T(8,128)(2,1)} %wo_ref.1), custom_call_target="tpu_custom_call" | custom-call | tf_op jit(solution)/shard_map/pallas_call | solution.py:442
  77.1 1.9 %copy.9 = bf16[128,2048]{1,0:T(8,128)(2,1)} copy(bf16[128,2048]{1,0:T(8,128)(2,1)} %shard_map.73) | data formatting | bytes 1048576
